TPU v7x, 32 devices: a whole 2x2x4 slice. The times are simulated.
32 devices in a mesh: row: 8 (over y, x, core), col: 4 (over z).
Axes of the slice: x: 2, y: 2, z: 4, core: 2. Of those that a mesh axis runs over, the one named last changes fastest.
Arguments:
- traces: bfloat16 [4096, 782], P(('row', 'col')), may hold values from -60 to 60
- taps: float32 [16], replicated, may hold values from -1.5 to 1.5
Outputs:
- correlations: float32 [32, 4096, 4096], P(None, 'row', 'col')
All inputs are finite; a program needn't handle non-finite values.
Results may differ from a plain program's by a relative error of at most 0.0036.
Values may be sent and summed in bfloat16 or wider, within the bound.
A program may use at most 256 MiB of HBM per device.

v0:
```python
import math
import jax
import jax.numpy as jnp
from jax import lax
from jax.sharding import PartitionSpec as P

LAGS = 32


def from_root(array, axis, root):
    mine = lax.axis_index(axis) == root
    return lax.psum(jnp.where(mine, array, jnp.zeros_like(array)), axis)


def whiten(traces, taps, count):
    samples = traces.astype(jnp.float32)
    decimated = jnp.zeros((samples.shape[0], count), jnp.float32)
    for k in range(taps.shape[0]):
        decimated = decimated + taps[k] * samples[:, k : k + 2 * count - 1 : 2]
    centred = decimated - jnp.mean(decimated, axis=1, keepdims=True)
    spread = jnp.sqrt(jnp.mean(centred * centred, axis=1, keepdims=True) + 1e-06)
    return (centred / spread).astype(jnp.bfloat16)


def on_device(traces, taps):
    count = (traces.shape[1] - taps.shape[0] + 2) // 2
    factor = lax.axis_size("row") // lax.axis_size("col")
    column = lax.axis_index("col")
    source = lax.all_gather(traces, "col", axis=0, tiled=True)
    first_block = whiten(source, taps, count)
    pieces = [from_root(source, "row", factor * column + k) for k in range(factor)]
    second_block = jnp.concatenate(pieces, axis=0)
    second_block = whiten(second_block, taps, count)
    lag_count = LAGS
    width = count - lag_count + 1
    scale_factor = 1.0 / math.sqrt(width)
    left = first_block[:, :width]
    groups = []
    for group in range(lag_count // 8):
        shifted = jnp.stack(
            [second_block[:, group * 8 + lag : group * 8 + lag + width] for lag in range(8)], axis=0
        )
        product = jnp.einsum("in,ljn->lij", left, shifted, preferred_element_type=jnp.float32)
        groups.append(product * scale_factor)
    return jnp.concatenate(groups, axis=0)


def solution(mesh):
    placed = (P(("row", "col"), None), P())
    return jax.shard_map(
        on_device, mesh=mesh, in_specs=placed, out_specs=P(None, "row", "col"), check_vma=False
    )
```

profile of v0, /device:TPU:0, one launch (start us, length us, event | category | flops | bytes accessed | tf_op | source)
XLA Modules:
  0.0 332.4 jit_solution(4783237983157764529)
XLA Ops:
  6.5 0.0 all-reduce.3.cloned.1.call-start
  6.5 20.8 %all_gather.3 = bf16[512,782]{0,1:T(8,128)(2,1)S(1)} all-gather(bf16[128,782]{0,1:T(8,128)(2,1)} %param.2), channel_id=1, replica_groups=mesh['row'=8,'col'=4] {'col'}, dimensions={0}, use_global_device_ids=true | all-gather | bytes 1000960 | tf_op jit(solution)/shard_map/all_gather | solution.py:29
  27.3 1.3 broadcast_select_fusion.1
  28.6 0.0 all-reduce.3.cloned.1.call-update
  28.6 0.9 slice.301
  29.5 0.9 slice.302
  30.4 0.9 slice.303
  31.3 2.9 slice.304
  34.2 2.8 slice.305
  37.1 2.8 slice.306
  39.9 2.8 slice.307
  42.7 2.8 slice.308
  45.5 2.8 slice.309
  48.4 2.9 slice.310
  51.2 2.9 slice.311
  54.1 2.9 slice.312
  57.0 2.9 slice.313
  59.8 2.8 slice.314
  62.6 2.8 slice.299
  65.4 2.8 slice.300
  68.2 0.0 copy-done.4
  68.2 0.7 fusion.39
  68.9 15.6 %fusion.37 = (f32[512]{0:T(512)S(1)}, f32[512,384]{0,1:T(8,128)S(1)}) fusion(f32[512,384]{0,1:T(8,128)} %slice.314, f32[]{:T(128)} %bitcast.15, f32[512,384]{0,1:T(8,128)} %slice.313, f32[]{:T(128)} %bitcast.14, f32[512,384]{0,1:T(8,128)} %slice.312, f32[]{:T(128)} %bitcast.13, f32[512,384]{0,1:T(8,128)} %slice.311, f32[]{:T(128)} %bitcast.12, ...), kind=kLoop, calls=%fused_computation.88 | loop fusion | flops 6290944 | bytes 13371456 | tf_op jit(solution)/shard_map/reduce_sum | solution.py:20
  84.5 0.1 multiply_reduce_fusion.1
  84.6 0.9 fusion.24
  85.5 1.4 all-reduce.3.cloned.1.call-done
  86.9 1.8 maximum_convert_fusion
  88.7 4.3 %slice.290 = f32[1024,384]{0,1:T(8,128)} slice(f32[1024,782]{0,1:T(8,128)S(1)} %maximum_convert_fusion), slice={[0:1024:1], [15:782:2]} | slice | bytes 3145728 | tf_op jit(solution)/shard_map/slice | solution.py:19
  93.0 4.3 %slice.288 = f32[1024,384]{0,1:T(8,128)} slice(f32[1024,782]{0,1:T(8,128)S(1)} %maximum_convert_fusion), slice={[0:1024:1], [14:781:2]} | slice | bytes 3145728 | tf_op jit(solution)/shard_map/slice | solution.py:19
  97.3 4.3 %slice.286 = f32[1024,384]{0,1:T(8,128)} slice(f32[1024,782]{0,1:T(8,128)S(1)} %maximum_convert_fusion), slice={[0:1024:1], [13:780:2]} | slice | bytes 3145728 | tf_op jit(solution)/shard_map/slice | solution.py:19
  101.6 4.3 %slice.284 = f32[1024,384]{0,1:T(8,128)} slice(f32[1024,782]{0,1:T(8,128)S(1)} %maximum_convert_fusion), slice={[0:1024:1], [12:779:2]} | slice | bytes 3145728 | tf_op jit(solution)/shard_map/slice | solution.py:19
  105.9 4.4 %slice.282 = f32[1024,384]{0,1:T(8,128)} slice(f32[1024,782]{0,1:T(8,128)S(1)} %maximum_convert_fusion), slice={[0:1024:1], [11:778:2]} | slice | bytes 3145728 | tf_op jit(solution)/shard_map/slice | solution.py:19
  110.2 4.3 %slice.280 = f32[1024,384]{0,1:T(8,128)} slice(f32[1024,782]{0,1:T(8,128)S(1)} %maximum_convert_fusion), slice={[0:1024:1], [10:777:2]} | slice | bytes 3145728 | tf_op jit(solution)/shard_map/slice | solution.py:19
  114.5 4.3 %slice.278 = f32[1024,384]{0,1:T(8,128)} slice(f32[1024,782]{0,1:T(8,128)S(1)} %maximum_convert_fusion), slice={[0:1024:1], [9:776:2]} | slice | bytes 3145728 | tf_op jit(solution)/shard_map/slice | solution.py:19
  118.8 4.2 %slice.276 = f32[1024,384]{0,1:T(8,128)} slice(f32[1024,782]{0,1:T(8,128)S(1)} %maximum_convert_fusion), slice={[0:1024:1], [8:775:2]} | slice | bytes 3145728 | tf_op jit(solution)/shard_map/slice | solution.py:19
  123.0 4.3 %slice.274 = f32[1024,384]{0,1:T(8,128)} slice(f32[1024,782]{0,1:T(8,128)S(1)} %maximum_convert_fusion), slice={[0:1024:1], [7:774:2]} | slice | bytes 3145728 | tf_op jit(solution)/shard_map/slice | solution.py:19
  127.3 4.3 %slice.272 = f32[1024,384]{0,1:T(8,128)} slice(f32[1024,782]{0,1:T(8,128)S(1)} %maximum_convert_fusion), slice={[0:1024:1], [6:773:2]} | slice | bytes 3145728 | tf_op jit(solution)/shard_map/slice | solution.py:19
  131.6 4.3 %slice.270 = f32[1024,384]{0,1:T(8,128)} slice(f32[1024,782]{0,1:T(8,128)S(1)} %maximum_convert_fusion), slice={[0:1024:1], [5:772:2]} | slice | bytes 3145728 | tf_op jit(solution)/shard_map/slice | solution.py:19
  135.9 4.3 %slice.268 = f32[1024,384]{0,1:T(8,128)} slice(f32[1024,782]{0,1:T(8,128)S(1)} %maximum_convert_fusion), slice={[0:1024:1], [4:771:2]} | slice | bytes 3145728 | tf_op jit(solution)/shard_map/slice | solution.py:19
  140.2 4.3 %slice.266 = f32[1024,384]{0,1:T(8,128)} slice(f32[1024,782]{0,1:T(8,128)S(1)} %maximum_convert_fusion), slice={[0:1024:1], [3:770:2]} | slice | bytes 3145728 | tf_op jit(solution)/shard_map/slice | solution.py:19
  144.6 4.3 %slice.264 = f32[1024,384]{0,1:T(8,128)} slice(f32[1024,782]{0,1:T(8,128)S(1)} %maximum_convert_fusion), slice={[0:1024:1], [2:769:2]} | slice | bytes 3145728 | tf_op jit(solution)/shard_map/slice | solution.py:19
  148.9 4.2 %slice.262 = f32[1024,384]{0,1:T(8,128)} slice(f32[1024,782]{0,1:T(8,128)S(1)} %maximum_convert_fusion), slice={[0:1024:1], [1:768:2]} | slice | bytes 3145728 | tf_op jit(solution)/shard_map/slice | solution.py:19
  153.1 4.2 %slice.260 = f32[1024,384]{0,1:T(8,128)} slice(f32[1024,782]{0,1:T(8,128)S(1)} %maximum_convert_fusion), slice={[0:1024:1], [0:767:2]} | slice | bytes 3145728 | tf_op jit(solution)/shard_map/slice | solution.py:19
  157.3 21.6 %fusion.38 = (f32[1024]{0:T(1024)S(1)}, f32[1024,384]{0,1:T(8,128)S(1)}) fusion(f32[1024,384]{0,1:T(8,128)} %slice.290, f32[]{:T(128)} %bitcast.15, f32[1024,384]{0,1:T(8,128)} %slice.288, f32[]{:T(128)} %bitcast.14, f32[1024,384]{0,1:T(8,128)} %slice.286, f32[]{:T(128)} %bitcast.13, f32[1024,384]{0,1:T(8,128)} %slice.284, f32[]{:T(128)} %bitcast.12, ...), kind=kLoop, calls=%fused_computation.89 | loop fusion | flops 12581888 | bytes 26742848 | tf_op jit(solution)/shard_map/reduce_sum | solution.py:20
  178.9 0.2 multiply_reduce_fusion
  179.2 0.2 divide_convert_fusion
  179.4 0.3 fusion.32
  179.7 0.4 fusion.31
  180.1 0.4 fusion.30
  180.5 0.4 fusion.29
  180.9 0.4 fusion.28
  181.3 0.4 fusion.27
  181.7 0.0 copy-start.3
  181.7 0.4 fusion.26
  182.1 0.4 fusion.25
  182.6 2.6 copy-done
  185.1 2.5 copy-done.2
  187.7 5.1 %multiply_bitcast_fusion.3 = f32[8,512,1024]{1,2,0:T(8,128)S(1)} fusion(bf16[8,1024,353]{1,2,0:T(8,128)(2,1)S(1)} %get-tuple-element.15, bf16[512,353]{0,1:T(8,128)(2,1)S(1)} %copy-done.3), kind=kOutput, calls=%fused_computation.4 | convolution fusion | flops 2965372928 | bytes 22922240 | tf_op jit(solution)/shard_map/in,ljn->lij/dot_general | solution.py:43
  192.8 0.0 slice-start
  192.8 9.0 %multiply_bitcast_fusion = f32[8,512,1024]{1,2,0:T(8,128)} fusion(bf16[8,1024,353]{1,2,0:T(8,128)(2,1)S(1)} %get-tuple-element.16, bf16[512,353]{0,1:T(8,128)(2,1)S(1)} %copy-done.3), kind=kOutput, calls=%fused_computation.1 | convolution fusion | flops 2965372928 | bytes 22922240 | tf_op jit(solution)/shard_map/in,ljn->lij/dot_general | solution.py:43
  201.9 8.5 %multiply_bitcast_fusion.1 = f32[8,512,1024]{1,2,0:T(8,128)} fusion(bf16[8,1024,353]{1,2,0:T(8,128)(2,1)S(1)} %copy-done.1, bf16[512,353]{0,1:T(8,128)(2,1)S(1)} %copy-done.3), kind=kOutput, calls=%fused_computation.2 | convolution fusion | flops 2965372928 | bytes 22922240 | tf_op jit(solution)/shard_map/in,ljn->lij/dot_general | solution.py:43
  210.4 8.5 %multiply_bitcast_fusion.2 = f32[8,512,1024]{1,2,0:T(8,128)} fusion(bf16[8,1024,353]{1,2,0:T(8,128)(2,1)S(1)} %bitcast.166, bf16[512,353]{0,1:T(8,128)(2,1)S(1)} %copy-done.3), kind=kOutput, calls=%fused_computation.3 | convolution fusion | flops 2965372928 | bytes 22922240 | tf_op jit(solution)/shard_map/in,ljn->lij/dot_general | solution.py:43
  218.8 40.9 %pad_maximum_fusion = f32[32,512,1024]{1,2,0:T(8,128)} fusion(f32[8,512,1024]{1,2,0:T(8,128)} %multiply_bitcast_fusion, f32[8,512,1024]{1,2,0:T(8,128)} %multiply_bitcast_fusion.1, f32[8,512,1024]{1,2,0:T(8,128)} %multiply_bitcast_fusion.2, f32[8,512,1024]{1,2,0:T(8,128)S(1)} %multiply_bitcast_fusion.3), kind=kLoop, calls=%fused_computation | loop fusion | flops 50331648 | bytes 134217728 | tf_op jit(solution)/shard_map/concatenate | solution.py:45
  259.7 65.8 %copy.3 = f32[32,512,1024]{2,1,0:T(8,128)} copy(f32[32,512,1024]{1,2,0:T(8,128)} %pad_maximum_fusion) | data formatting | bytes 134217728 | tf_op jit(solution)/shard_map/concatenate | solution.py:45
  (14 shorter events, 0.0 us)
Async XLA Ops:
  6.5 80.3 %all-reduce.3.cloned.1.call-start = ((), (), s32[]{:S(2)}) async-start(), calls=%async_computation | async-start | bytes 3211264 | tf_op jit(solution)/shard_map/psum | solution.py:12
  48.4 19.8 %copy-start.4 = (f32[16]{0:T(128)S(1)}, f32[16]{0:T(128)}, u32[]{:S(2)}) copy-start(f32[16]{0:T(128)} %param.3) | copy-start | bytes 196
  181.7 5.9 %copy-start.3 = (bf16[512,353]{0,1:T(8,128)(2,1)S(1)}, bf16[512,353]{0,1:T(8,128)(2,1)}, u32[]{:S(2)}) copy-start(bf16[512,353]{0,1:T(8,128)(2,1)} %fusion.24) | copy-start | bytes 1084420
  182.5 2.6 copy-start
  185.1 2.5 copy-start.2
  192.8 9.1 %copy-start.1 = (bf16[8,1024,353]{1,2,0:T(8,128)(2,1)S(1)}, bf16[8,1024,353]{1,2,0:T(8,128)(2,1)}, u32[]{:S(2)}) copy-start(bf16[8,1024,353]{1,2,0:T(8,128)(2,1)} %copy-done) | copy-start | bytes 17350660
  192.8 17.5 %slice-start = ((s8[5898240]{0:T(1024)(128)(4,1)}), s8[1703936]{0:T(1024)(128)(4,1)S(1)}, s32[]{:S(2)}) async-start(s8[5898240]{0:T(1024)(128)(4,1)} %bitcast.165), calls=%async_computation.1 | async-start | bytes 3407872
  201.9 8.5 %slice-start.1 = ((s8[5898240]{0:T(1024)(128)(4,1)}), s8[4194304]{0:T(1024)(128)(4,1)S(1)}, s32[]{:S(2)}) async-start(s8[5898240]{0:T(1024)(128)(4,1)} %bitcast.165), calls=%async_computation.2 | async-start | bytes 8388608
Sparse Core Ops, SparseCore 0:
  28.8 58.0 all-reduce.2
where the time goes:
time: 334 us; the launch traced here: 332 us
  local copies, waits for them, and re-layouts  183 us (55%)
  other arithmetic  82.7 us (25%)
  matrix products  31.1 us (9%)
  blocking collectives  20.8 us (6%)
  between operations  13.6 us (4%)
    slice x33, local copies, waits for them, and re-layouts, whiten(): decimated = decimated + taps[k] * samples[:, k:k + 2 * count - 1:2]  109 us
    concatenate x1, local copies, waits for them, and re-layouts, on_device(): return jnp.concatenate(groups, axis=0)  65.8 us
    concatenate x1, other arithmetic, on_device(): return jnp.concatenate(groups, axis=0)  40.9 us
    reduce_sum x2, other arithmetic, whiten(): centred = decimated - jnp.mean(decimated, axis=1, keepdims=True)  37.2 us
    dot_general x4, matrix products, on_device(): jnp.einsum('in,ljn->lij', left, shifted, preferred_element_type=jnp.float32)  31.1 us
    all_gather x1, blocking collectives, on_device(): source = lax.all_gather(traces, 'col', axis=0, tiled=True)  20.8 us
    unnamed x21, local copies, waits for them, and re-layouts  7.78 us
  transfers between devices with their start and end apart: 1, of which 1 were waited for; matrix products, arithmetic and copies ran while one was open for 17% of the time, Pallas kernels for 0%

commit v1 on v0

--- a/solution.py
+++ b/solution.py
@@ -5,6 +5,18 @@
 from jax.sharding import PartitionSpec as P
 
 LAGS = 32
+
+
+def gather_by_bits(x, axis, dim):
+    ways, here, lap = (lax.axis_size(axis), lax.axis_index(axis), x.shape[dim])
+    line, have = (x, 1)
+    while have < ways:
+        line = jnp.concatenate(
+            [line, lax.ppermute(line, axis, [(d, (d - have) % ways) for d in range(ways)])],
+            axis=dim,
+        )
+        have = 2 * have
+    return jnp.roll(line, here * lap, axis=dim)
 
 
 def from_root(array, axis, root):
@@ -26,7 +38,7 @@
     count = (traces.shape[1] - taps.shape[0] + 2) // 2
     factor = lax.axis_size("row") // lax.axis_size("col")
     column = lax.axis_index("col")
-    source = lax.all_gather(traces, "col", axis=0, tiled=True)
+    source = gather_by_bits(traces, "col", 0)
     first_block = whiten(source, taps, count)
     pieces = [from_root(source, "row", factor * column + k) for k in range(factor)]
     second_block = jnp.concatenate(pieces, axis=0)

time: 334 us -> 386 us (1.16)
  waiting for transfers between devices: 1.4 us -> 62.4 us
  blocking collectives: 20.8 us -> 0 us
  starting transfers between devices: 0.01 us -> 6.48 us
  local copies, waits for them, and re-layouts: 183 us -> 187 us
    psum x1, waiting for transfers between devices: 1.39 us -> 42.5 us  [from_root(): return lax.psum(jnp.where(mine, array, jnp.zeros_like(array)), axis)]
    all_gather x1 -> x0, blocking collectives: 20.8 us -> none  [on_device(): source = lax.all_gather(traces, 'col', axis=0, tiled=True)]
    ppermute x0 -> x2, waiting for transfers between devices: none -> 19.8 us  [gather_by_bits(): lax.ppermute(line, axis, [(d, (d - have) % ways) for d in range(ways)])]
    ppermute x0 -> x2, starting transfers between devices: none -> 6.48 us  [gather_by_bits(): lax.ppermute(line, axis, [(d, (d - have) % ways) for d in range(ways)])]
    unnamed x21 -> x24, local copies, waits for them, and re-layouts: 7.78 us -> 9.91 us
  transfers between devices with their start and end apart: 1 -> 3, of which waited for: 1 -> 3; matrix products, arithmetic and copies ran while one was open for 17% -> 5% of each run, Pallas kernels for 0% -> 0%
where the time goes in v1:
time: 386 us; the launch traced here: 385 us
  local copies, waits for them, and re-layouts  187 us (48%)
  other arithmetic  84.2 us (22%)
  waiting for transfers between devices  62.4 us (16%)
  matrix products  31.1 us (8%)
  between operations  13.6 us (4%)
  starting transfers between devices  6.48 us (2%)
    slice x33, local copies, waits for them, and re-layouts, whiten(): decimated = decimated + taps[k] * samples[:, k:k + 2 * count - 1:2]  111 us
    concatenate x1, local copies, waits for them, and re-layouts, on_device(): return jnp.concatenate(groups, axis=0)  65.8 us
    psum x1, waiting for transfers between devices, from_root(): return lax.psum(jnp.where(mine, array, jnp.zeros_like(array)), axis)  42.5 us
    concatenate x1, other arithmetic, on_device(): return jnp.concatenate(groups, axis=0)  40.9 us
    reduce_sum x2, other arithmetic, whiten(): centred = decimated - jnp.mean(decimated, axis=1, keepdims=True)  37.5 us
    dot_general x4, matrix products, on_device(): jnp.einsum('in,ljn->lij', left, shifted, preferred_element_type=jnp.float32)  31.1 us
    ppermute x2, waiting for transfers between devices, gather_by_bits(): lax.ppermute(line, axis, [(d, (d - have) % ways) for d in range(ways)])  19.8 us
    unnamed x24, local copies, waits for them, and re-layouts  9.91 us
  transfers between devices with their start and end apart: 3, of which 3 were waited for; matrix products, arithmetic and copies ran while one was open for 5% of the time, Pallas kernels for 0%

profile of v1, /device:TPU:0, one launch (start us, length us, event | category | flops | bytes accessed | tf_op | source)
XLA Modules:
  0.0 384.7 jit_solution(11215123368041567695)
XLA Ops:
  6.5 5.0 %collective-permute-start = (bf16[128,782]{0,1:T(8,128)(2,1)}, bf16[128,782]{0,1:T(8,128)(2,1)S(1)}, u32[]{:S(2)}, u32[]{:S(2)}) collective-permute-start(bf16[128,782]{0,1:T(8,128)(2,1)} %param.2), channel_id=1, source_target_pairs={{0,3},{1,0},{2,1},{3,2},{4,7},{5,4},{6,5},{7,6},{8,11},{9,8},{10,9... | collective-permute-start | bytes 600584 | tf_op jit(solution)/shard_map/ppermute | solution.py:15
  11.6 4.6 %collective-permute-done = bf16[128,782]{0,1:T(8,128)(2,1)S(1)} collective-permute-done((bf16[128,782]{0,1:T(8,128)(2,1)}, bf16[128,782]{0,1:T(8,128)(2,1)S(1)}, u32[]{:S(2)}, u32[]{:S(2)}) %collective-permute-start) | collective-permute-done | bytes 200224 | tf_op jit(solution)/shard_map/ppermute | solution.py:15
  16.2 1.0 pad_maximum_fusion.1
  17.1 1.4 collective-permute-start.1
  18.6 2.0 fusion.39
  20.5 1.0 constant_dynamic-update-slice_fusion.5
  21.6 15.3 %collective-permute-done.1 = bf16[256,782]{0,1:T(8,128)(2,1)S(1)} collective-permute-done((bf16[256,782]{0,1:T(8,128)(2,1)S(1)}, bf16[256,782]{0,1:T(8,128)(2,1)S(1)}, u32[]{:S(2)}, u32[]{:S(2)}) %collective-permute-start.1) | collective-permute-done | bytes 400416 | tf_op jit(solution)/shard_map/ppermute | solution.py:15
  36.9 1.0 constant_dynamic-update-slice_fusion.2
  38.0 1.6 dynamic-slice_convert_fusion
  39.6 0.7 slice.314
  40.4 0.8 slice.313
  41.1 2.8 slice.312
  43.9 2.8 slice.311
  46.8 2.8 slice.310
  49.6 2.8 slice.309
  52.4 2.8 slice.308
  55.2 2.8 slice.307
  58.0 2.8 slice.306
  60.8 2.8 slice.305
  63.6 2.8 slice.304
  66.4 2.8 slice.303
  69.2 2.8 slice.302
  72.0 2.8 slice.301
  74.8 2.7 slice.300
  77.5 2.7 slice.299
  80.3 15.9 %fusion.37 = (f32[512]{0:T(512)S(1)}, f32[512,384]{0,1:T(8,128)S(1)}) fusion(f32[512,384]{0,1:T(8,128)S(1)} %slice.314, f32[]{:T(128)} %bitcast.15, f32[512,384]{0,1:T(8,128)S(1)} %slice.313, f32[]{:T(128)} %bitcast.14, f32[512,384]{0,1:T(8,128)} %slice.312, f32[]{:T(128)} %bitcast.13, f32[512,384]{0,1:T(8,128)} %slice.311, f32[]{:T(128)} %bitcast.12, ...), kind=kLoop, calls=%fused_computation.96 | loop fusion | flops 6290944 | bytes 13371456 | tf_op jit(solution)/shard_map/reduce_sum | solution.py:32
  96.3 0.8 fusion.24
  97.2 42.5 %all-reduce.3.cloned.1.call-done = (bf16[512,782]{0,1:T(8,128)(2,1)}, bf16[512,782]{0,1:T(8,128)(2,1)}) async-done(((bf16[512,782]{0,1:T(8,128)(2,1)}, bf16[512,782]{0,1:T(8,128)(2,1)}), (bf16[512,782]{0,1:T(8,128)(2,1)}, bf16[512,782]{0,1:T(8,128)(2,1)})) %all-reduce.3.cloned.1.call-update) | async-done | bytes 1601552 | tf_op jit(solution)/shard_map/psum | solution.py:24
  139.7 1.8 maximum_convert_fusion
  141.5 4.3 %slice.290 = f32[1024,384]{0,1:T(8,128)} slice(f32[1024,782]{0,1:T(8,128)S(1)} %maximum_convert_fusion), slice={[0:1024:1], [15:782:2]} | slice | bytes 3145728 | tf_op jit(solution)/shard_map/slice | solution.py:31
  145.8 4.3 %slice.288 = f32[1024,384]{0,1:T(8,128)} slice(f32[1024,782]{0,1:T(8,128)S(1)} %maximum_convert_fusion), slice={[0:1024:1], [14:781:2]} | slice | bytes 3145728 | tf_op jit(solution)/shard_map/slice | solution.py:31
  150.0 4.3 %slice.286 = f32[1024,384]{0,1:T(8,128)} slice(f32[1024,782]{0,1:T(8,128)S(1)} %maximum_convert_fusion), slice={[0:1024:1], [13:780:2]} | slice | bytes 3145728 | tf_op jit(solution)/shard_map/slice | solution.py:31
  154.3 4.3 %slice.284 = f32[1024,384]{0,1:T(8,128)} slice(f32[1024,782]{0,1:T(8,128)S(1)} %maximum_convert_fusion), slice={[0:1024:1], [12:779:2]} | slice | bytes 3145728 | tf_op jit(solution)/shard_map/slice | solution.py:31
  158.6 4.3 %slice.282 = f32[1024,384]{0,1:T(8,128)} slice(f32[1024,782]{0,1:T(8,128)S(1)} %maximum_convert_fusion), slice={[0:1024:1], [11:778:2]} | slice | bytes 3145728 | tf_op jit(solution)/shard_map/slice | solution.py:31
  162.9 4.3 %slice.280 = f32[1024,384]{0,1:T(8,128)} slice(f32[1024,782]{0,1:T(8,128)S(1)} %maximum_convert_fusion), slice={[0:1024:1], [10:777:2]} | slice | bytes 3145728 | tf_op jit(solution)/shard_map/slice | solution.py:31
  167.2 4.2 %slice.278 = f32[1024,384]{0,1:T(8,128)} slice(f32[1024,782]{0,1:T(8,128)S(1)} %maximum_convert_fusion), slice={[0:1024:1], [9:776:2]} | slice | bytes 3145728 | tf_op jit(solution)/shard_map/slice | solution.py:31
  171.4 4.2 %slice.276 = f32[1024,384]{0,1:T(8,128)} slice(f32[1024,782]{0,1:T(8,128)S(1)} %maximum_convert_fusion), slice={[0:1024:1], [8:775:2]} | slice | bytes 3145728 | tf_op jit(solution)/shard_map/slice | solution.py:31
  175.6 4.2 %slice.274 = f32[1024,384]{0,1:T(8,128)} slice(f32[1024,782]{0,1:T(8,128)S(1)} %maximum_convert_fusion), slice={[0:1024:1], [7:774:2]} | slice | bytes 3145728 | tf_op jit(solution)/shard_map/slice | solution.py:31
  179.8 4.3 %slice.272 = f32[1024,384]{0,1:T(8,128)} slice(f32[1024,782]{0,1:T(8,128)S(1)} %maximum_convert_fusion), slice={[0:1024:1], [6:773:2]} | slice | bytes 3145728 | tf_op jit(solution)/shard_map/slice | solution.py:31
  184.1 4.3 %slice.270 = f32[1024,384]{0,1:T(8,128)} slice(f32[1024,782]{0,1:T(8,128)S(1)} %maximum_convert_fusion), slice={[0:1024:1], [5:772:2]} | slice | bytes 3145728 | tf_op jit(solution)/shard_map/slice | solution.py:31
  188.4 4.3 %slice.268 = f32[1024,384]{0,1:T(8,128)} slice(f32[1024,782]{0,1:T(8,128)S(1)} %maximum_convert_fusion), slice={[0:1024:1], [4:771:2]} | slice | bytes 3145728 | tf_op jit(solution)/shard_map/slice | solution.py:31
  192.7 4.3 %slice.266 = f32[1024,384]{0,1:T(8,128)} slice(f32[1024,782]{0,1:T(8,128)S(1)} %maximum_convert_fusion), slice={[0:1024:1], [3:770:2]} | slice | bytes 3145728 | tf_op jit(solution)/shard_map/slice | solution.py:31
  197.0 4.3 %slice.264 = f32[1024,384]{0,1:T(8,128)} slice(f32[1024,782]{0,1:T(8,128)S(1)} %maximum_convert_fusion), slice={[0:1024:1], [2:769:2]} | slice | bytes 3145728 | tf_op jit(solution)/shard_map/slice | solution.py:31
  201.3 4.2 %slice.262 = f32[1024,384]{0,1:T(8,128)} slice(f32[1024,782]{0,1:T(8,128)S(1)} %maximum_convert_fusion), slice={[0:1024:1], [1:768:2]} | slice | bytes 3145728 | tf_op jit(solution)/shard_map/slice | solution.py:31
  205.4 4.2 %slice.260 = f32[1024,384]{0,1:T(8,128)} slice(f32[1024,782]{0,1:T(8,128)S(1)} %maximum_convert_fusion), slice={[0:1024:1], [0:767:2]} | slice | bytes 3145728 | tf_op jit(solution)/shard_map/slice | solution.py:31
  209.6 21.6 %fusion.38 = (f32[1024]{0:T(1024)S(1)}, f32[1024,384]{0,1:T(8,128)S(1)}) fusion(f32[1024,384]{0,1:T(8,128)} %slice.290, f32[]{:T(128)} %bitcast.15, f32[1024,384]{0,1:T(8,128)} %slice.288, f32[]{:T(128)} %bitcast.14, f32[1024,384]{0,1:T(8,128)} %slice.286, f32[]{:T(128)} %bitcast.13, f32[1024,384]{0,1:T(8,128)} %slice.284, f32[]{:T(128)} %bitcast.12, ...), kind=kLoop, calls=%fused_computation.97 | loop fusion | flops 12581888 | bytes 26742848 | tf_op jit(solution)/shard_map/reduce_sum | solution.py:32
  231.3 0.2 multiply_reduce_fusion
  231.5 0.2 divide_convert_fusion
  231.7 0.3 fusion.32
  232.1 0.4 fusion.31
  232.5 0.4 fusion.30
  232.9 0.4 fusion.29
  233.3 0.4 fusion.28
  233.7 0.4 fusion.27
  234.1 0.4 fusion.26
  234.5 0.4 fusion.25
  234.9 2.6 copy-done
  237.4 2.5 copy-done.2
  240.0 5.1 %multiply_bitcast_fusion.3 = f32[8,512,1024]{1,2,0:T(8,128)S(1)} fusion(bf16[8,1024,353]{1,2,0:T(8,128)(2,1)S(1)} %get-tuple-element.16, bf16[512,353]{0,1:T(8,128)(2,1)S(1)} %copy-done.3), kind=kOutput, calls=%fused_computation.4 | convolution fusion | flops 2965372928 | bytes 22922240 | tf_op jit(solution)/shard_map/in,ljn->lij/dot_general | solution.py:55
  245.1 9.0 %multiply_bitcast_fusion = f32[8,512,1024]{1,2,0:T(8,128)} fusion(bf16[8,1024,353]{1,2,0:T(8,128)(2,1)S(1)} %get-tuple-element.17, bf16[512,353]{0,1:T(8,128)(2,1)S(1)} %copy-done.3), kind=kOutput, calls=%fused_computation.1 | convolution fusion | flops 2965372928 | bytes 22922240 | tf_op jit(solution)/shard_map/in,ljn->lij/dot_general | solution.py:55
  254.2 8.5 %multiply_bitcast_fusion.1 = f32[8,512,1024]{1,2,0:T(8,128)} fusion(bf16[8,1024,353]{1,2,0:T(8,128)(2,1)S(1)} %copy-done.1, bf16[512,353]{0,1:T(8,128)(2,1)S(1)} %copy-done.3), kind=kOutput, calls=%fused_computation.2 | convolution fusion | flops 2965372928 | bytes 22922240 | tf_op jit(solution)/shard_map/in,ljn->lij/dot_general | solution.py:55
  262.7 8.5 %multiply_bitcast_fusion.2 = f32[8,512,1024]{1,2,0:T(8,128)} fusion(bf16[8,1024,353]{1,2,0:T(8,128)(2,1)S(1)} %bitcast.166, bf16[512,353]{0,1:T(8,128)(2,1)S(1)} %copy-done.3), kind=kOutput, calls=%fused_computation.3 | convolution fusion | flops 2965372928 | bytes 22922240 | tf_op jit(solution)/shard_map/in,ljn->lij/dot_general | solution.py:55
  271.1 40.9 %pad_maximum_fusion = f32[32,512,1024]{1,2,0:T(8,128)} fusion(f32[8,512,1024]{1,2,0:T(8,128)} %multiply_bitcast_fusion, f32[8,512,1024]{1,2,0:T(8,128)} %multiply_bitcast_fusion.1, f32[8,512,1024]{1,2,0:T(8,128)} %multiply_bitcast_fusion.2, f32[8,512,1024]{1,2,0:T(8,128)S(1)} %multiply_bitcast_fusion.3), kind=kLoop, calls=%fused_computation | loop fusion | flops 50331648 | bytes 134217728 | tf_op jit(solution)/shard_map/concatenate | solution.py:57
  312.0 65.8 %copy.3 = f32[32,512,1024]{2,1,0:T(8,128)} copy(f32[32,512,1024]{1,2,0:T(8,128)} %pad_maximum_fusion) | data formatting | bytes 134217728 | tf_op jit(solution)/shard_map/concatenate | solution.py:57
  (22 shorter events, 0.4 us)
Async XLA Ops:
  6.5 133.1 %all-reduce.3.cloned.1.call-start = ((), (), s32[]{:S(2)}) async-start(), calls=%async_computation | async-start | bytes 3211264 | tf_op jit(solution)/shard_map/psum | solution.py:24
  6.5 9.6 %collective-permute-start = (bf16[128,782]{0,1:T(8,128)(2,1)}, bf16[128,782]{0,1:T(8,128)(2,1)S(1)}, u32[]{:S(2)}, u32[]{:S(2)}) collective-permute-start(bf16[128,782]{0,1:T(8,128)(2,1)} %param.2), channel_id=1, source_target_pairs={{0,3},{1,0},{2,1},{3,2},{4,7},{5,4},{6,5},{7,6},{8,11},{9,8},{10,9... | collective-permute-start | bytes 600584 | tf_op jit(solution)/shard_map/ppermute | solution.py:15
  17.1 19.7 %collective-permute-start.1 = (bf16[256,782]{0,1:T(8,128)(2,1)S(1)}, bf16[256,782]{0,1:T(8,128)(2,1)S(1)}, u32[]{:S(2)}, u32[]{:S(2)}) collective-permute-start(bf16[256,782]{0,1:T(8,128)(2,1)S(1)} %pad_maximum_fusion.1), channel_id=1, source_target_pairs={{0,2},{1,3},{2,0},{3,1},{4,6},{5,7},{6,4},{7,5},{8,10},{9,11},{10,... | collective-permute-start | bytes 1201160 | tf_op jit(solution)/shard_map/ppermute | solution.py:15
  234.1 5.9 %copy-start.3 = (bf16[512,353]{0,1:T(8,128)(2,1)S(1)}, bf16[512,353]{0,1:T(8,128)(2,1)}, u32[]{:S(2)}) copy-start(bf16[512,353]{0,1:T(8,128)(2,1)} %fusion.24) | copy-start | bytes 1084420
  234.9 2.6 copy-start
  237.4 2.5 copy-start.2
  245.1 9.1 %copy-start.1 = (bf16[8,1024,353]{1,2,0:T(8,128)(2,1)S(1)}, bf16[8,1024,353]{1,2,0:T(8,128)(2,1)}, u32[]{:S(2)}) copy-start(bf16[8,1024,353]{1,2,0:T(8,128)(2,1)} %copy-done) | copy-start | bytes 17350660
  245.1 17.5 %slice-start = ((s8[5898240]{0:T(1024)(128)(4,1)}), s8[1703936]{0:T(1024)(128)(4,1)S(1)}, s32[]{:S(2)}) async-start(s8[5898240]{0:T(1024)(128)(4,1)} %bitcast.165), calls=%async_computation.1 | async-start | bytes 3407872
  254.2 8.5 %slice-start.1 = ((s8[5898240]{0:T(1024)(128)(4,1)}), s8[4194304]{0:T(1024)(128)(4,1)S(1)}, s32[]{:S(2)}) async-start(s8[5898240]{0:T(1024)(128)(4,1)} %bitcast.165), calls=%async_computation.2 | async-start | bytes 8388608
Sparse Core Ops, SparseCore 0:
  80.4 59.2 all-reduce.2
